TPU v7x, 32 devices: a whole 2x2x4 slice. The times are simulated.
32 devices in a mesh: line: 8 (over z, core), scan: 4 (over y, x).
Axes of the slice: x: 2, y: 2, z: 4, core: 2. Of those that a mesh axis runs over, the one named last changes fastest.
Arguments:
- query_row: bfloat16 [8, 512, 512], P('line', 'scan'), may hold values from -6 to 6
- key_row: bfloat16 [8, 512, 512], P('line', 'scan'), may hold values from -6 to 6
- value_row: bfloat16 [8, 512, 512], P('line', 'scan'), may hold values from -6 to 6
- decay_row: float32 [8, 512, 4], P('line', 'scan'), may hold values from -2 to 0
- beta_row: float32 [8, 512, 4], P('line', 'scan'), may hold values from 0.02 to 0.2
- gain_row: float32 [128], replicated, may hold values from 0.1 to 1.9
- query_col: bfloat16 [8, 4, 128, 512], P(None, 'scan', 'line'), may hold values from -6 to 6
- key_col: bfloat16 [8, 4, 128, 512], P(None, 'scan', 'line'), may hold values from -6 to 6
- decay_col: float32 [8, 4, 128, 4], P(None, 'scan', 'line'), may hold values from -2 to 0
- beta_col: float32 [8, 4, 128, 4], P(None, 'scan', 'line'), may hold values from 0.02 to 0.2
- gain_col: float32 [128], replicated, may hold values from 0.1 to 1.9
Outputs:
- mixed: bfloat16 [8, 512, 512], P('line', 'scan')
All inputs are finite; a program needn't handle non-finite values.
Results may differ from a plain program's by a relative error of at most 0.0049.
Values may be sent and summed in bfloat16 or wider, within the bound.
A program may use at most 64 MiB of HBM per device.

v0:
```python
import jax
import jax.numpy as jnp
from jax import lax
from jax.sharding import PartitionSpec as P

HIGHEST = lax.Precision.HIGHEST


def from_behind(block, axis, distance):
    devices = range(lax.axis_size(axis))
    route = [(i - distance, i) for i in devices if i - distance in devices]
    return lax.ppermute(block, axis, route)


def block_terms(query_block, key_block, value_block, log_decay, beta_block):
    key_unit = key_block / jnp.sqrt(jnp.sum(key_block * key_block, axis=-1, keepdims=True) + 1e-06)
    cumulative = jnp.cumsum(log_decay, axis=-1)
    sequence_length = key_block.shape[1]
    lower_mask = jnp.tril(jnp.ones((sequence_length, sequence_length), dtype=jnp.bool_))
    strict = jnp.tril(jnp.ones((sequence_length, sequence_length), dtype=jnp.bool_), -1)
    spread = cumulative[:, :, None] - cumulative[:, None, :]
    ratios = jnp.where(lower_mask, jnp.exp(jnp.where(lower_mask, spread, 0.0)), 0.0)
    key_inner = jnp.einsum("bik,bjk->bij", key_unit, key_unit, precision=HIGHEST)
    system = jnp.where(strict, beta_block[:, :, None] * ratios * key_inner, 0.0) + jnp.eye(
        sequence_length, dtype=jnp.float32
    )
    growth = jnp.exp(cumulative)
    right_side = jnp.concatenate(
        [beta_block[:, :, None] * value_block, (beta_block * growth)[:, :, None] * key_unit],
        axis=-1,
    )
    solved = jax.scipy.linalg.solve_triangular(system, right_side, lower=True)
    value_size = value_block.shape[-1]
    updates = solved[:, :, :value_size]
    weighted = solved[:, :, value_size:]
    attend = ratios * jnp.einsum("bik,bjk->bij", query_block, key_unit, precision=HIGHEST)
    local_out = jnp.einsum("bij,bjv->biv", attend, updates, precision=HIGHEST)
    state_query = growth[:, :, None] * query_block - jnp.einsum(
        "bij,bjk->bik", attend, weighted, precision=HIGHEST
    )
    key_tail = jnp.exp(cumulative[:, -1:] - cumulative)[:, :, None] * key_unit
    return (local_out, state_query, key_tail, weighted, updates, growth[:, -1])


def scan_blocks(queries, key_rows, values, log_decay, beta_rows, block_extent):
    batch_size, sequence_length, head_size = queries.shape
    number_of_blocks = sequence_length // block_extent

    def blocks(array):
        return array.reshape(
            (batch_size, number_of_blocks, block_extent) + array.shape[2:]
        ).swapaxes(0, 1)

    def scan_advance(carried, pieces):
        local_out, state_query, key_tail, weighted, updates, ending = block_terms(*pieces)
        output = local_out + jnp.einsum("bik,bkv->biv", state_query, carried, precision=HIGHEST)
        residue = updates - jnp.einsum("bjk,bkv->bjv", weighted, carried, precision=HIGHEST)
        carried = ending[:, None, None] * carried + jnp.einsum(
            "bjk,bjv->bkv", key_tail, residue, precision=HIGHEST
        )
        return (carried, output)

    initial = jnp.zeros((batch_size, head_size, head_size), dtype=jnp.float32)
    last_state, outputs = lax.scan(
        scan_advance,
        initial,
        (blocks(queries), blocks(key_rows), blocks(values), blocks(log_decay), blocks(beta_rows)),
    )
    return outputs.swapaxes(0, 1).reshape(batch_size, sequence_length, head_size)


def to_heads(array, leading_count, sequence_length, head_count, head_size):
    shaped = array.astype(jnp.float32).reshape(
        leading_count, sequence_length, head_count, head_size
    )
    return shaped.transpose(0, 2, 1, 3).reshape(
        leading_count * head_count, sequence_length, head_size
    )


def gates_to_heads(array, leading_count, sequence_length, head_count):
    return array.transpose(0, 2, 1).reshape(leading_count * head_count, sequence_length)


def from_heads(array, leading_count, sequence_length, head_count, head_size):
    return array.reshape(leading_count, head_count, sequence_length, head_size).transpose(
        0, 2, 1, 3
    )


def head_norm(array, gain):
    return array * lax.rsqrt(jnp.mean(array * array, axis=-1, keepdims=True) + 1e-05) * gain


def shards(
    query_row,
    key_row,
    value_row,
    decay_row,
    beta_row,
    gain_row,
    query_col,
    key_col,
    decay_col,
    beta_col,
    gain_col,
):
    row_count, segment, features = query_row.shape
    head_size = gain_row.shape[0]
    head_count = features // head_size
    line_count = lax.axis_size("line")
    local_out, state_query, key_tail, weighted, updates, ending = block_terms(
        to_heads(query_row, row_count, segment, head_count, head_size),
        to_heads(key_row, row_count, segment, head_count, head_size),
        to_heads(value_row, row_count, segment, head_count, head_size),
        gates_to_heads(decay_row, row_count, segment, head_count),
        gates_to_heads(beta_row, row_count, segment, head_count),
    )
    identity = jnp.broadcast_to(
        jnp.eye(head_size, dtype=jnp.float32), (row_count * head_count, head_size, head_size)
    )
    transfer = ending[:, None, None] * identity - jnp.einsum(
        "bjk,bjl->bkl", key_tail, weighted, precision=HIGHEST
    )
    offset = jnp.einsum("bjk,bjv->bkv", key_tail, updates, precision=HIGHEST)

    def body_advance(number, carried):
        arrived = from_behind(carried[1], "scan", 1)
        return (arrived, jnp.einsum("bij,bjv->biv", transfer, arrived, precision=HIGHEST) + offset)

    incoming, leaving = lax.fori_loop(
        0, lax.axis_size("scan") - 1, body_advance, (jnp.zeros_like(offset), offset)
    )
    row_out = local_out + jnp.einsum("bik,bkv->biv", state_query, incoming, precision=HIGHEST)
    row_scan = from_heads(row_out, row_count, segment, head_count, head_size)
    values_col = (
        head_norm(row_scan, gain_row).reshape(row_count, segment, features).astype(jnp.bfloat16)
    )
    arranged = values_col.reshape(row_count, line_count, segment // line_count, features)
    column_values = lax.all_to_all(arranged, "line", split_axis=1, concat_axis=0, tiled=True)
    total_rows = query_col.shape[0]
    column_count = query_col.shape[2]

    def columns(array):
        return array.reshape(total_rows, column_count, -1).transpose(1, 0, 2)

    block_extent = min(segment, total_rows)
    col_out = scan_blocks(
        to_heads(columns(query_col), column_count, total_rows, head_count, head_size),
        to_heads(columns(key_col), column_count, total_rows, head_count, head_size),
        to_heads(columns(column_values), column_count, total_rows, head_count, head_size),
        gates_to_heads(columns(decay_col), column_count, total_rows, head_count),
        gates_to_heads(columns(beta_col), column_count, total_rows, head_count),
        block_extent,
    )
    col_scan = from_heads(col_out, column_count, total_rows, head_count, head_size)
    normed = (
        head_norm(col_scan, gain_col)
        .transpose(1, 0, 2, 3)
        .reshape(total_rows, 1, column_count, features)
        .astype(jnp.bfloat16)
    )
    returned = lax.all_to_all(normed, "line", split_axis=0, concat_axis=1, tiled=True)
    return returned.reshape(row_count, segment, features)


def solution(mesh):
    placed = (
        P("line", "scan", None),
        P("line", "scan", None),
        P("line", "scan", None),
        P("line", "scan", None),
        P("line", "scan", None),
        P(),
        P(None, "scan", "line", None),
        P(None, "scan", "line", None),
        P(None, "scan", "line", None),
        P(None, "scan", "line", None),
        P(),
    )
    return jax.shard_map(
        shards, mesh=mesh, in_specs=placed, out_specs=P("line", "scan", None), check_vma=False
    )
```

profile of v0, /device:TPU:5, one launch (start us, length us, event | category | flops | bytes accessed | tf_op | source)
XLA Modules:
  0.0 106.8 jit_solution(10542739660594414009)
XLA Ops:
  0.0 0.9 fusion.47
  0.9 0.8 fusion.44
  2.0 0.7 copy-done.2
  3.3 0.8 fusion.9
  4.1 39.3 %custom-call.10 = f32[4,1,128,128]{2,3,1,0:T(8,128)S(1)} custom-call(f32[4,1,128,128]{3,2,1,0:T(8,128)S(1)} %fusion.9), custom_call_target="InvertDiagBlocksLowerTriangular" | custom-call | tf_op jit(solution)/shard_map/jit(_solve_triangular)/vmap()/triangular_solve | solution.py:32
  43.9 0.6 fusion.10
  44.6 0.7 fusion.27
  45.3 0.7 convolution_subtract_fusion.1
  46.1 0.5 convolution_multiply_fusion.1
  46.6 0.6 fusion.29
  47.2 0.4 convolution_subtract_fusion.2
  47.6 29.1 %while.3 = (s32[]{:T(128)}, f32[4,128,128]{2,1,0:T(8,128)}, f32[4,128,128]{2,1,0:T(8,128)S(1)}, f32[4,128,128]{2,1,0:T(8,128)S(1)}, f32[4,128,128]{2,1,0:T(8,128)S(1)}) while((s32[]{:T(128)}, f32[4,128,128]{2,1,0:T(8,128)}, f32[4,128,128]{2,1,0:T(8,128)S(1)}, f32[4,128,128]{2,1,0:T(8,128)S(1)}, f32[4,128,128]{2,1,0:T(8,128)S(1)}) %tuple.55), condition=%wide.region_5.6_spmd.clone, body=%wide.region_4.5_spmd.sunk.clone | while | flops 100728832 | bytes 3145857 | solution.py:131
  47.7 3.1 %collective-permute-start = (f32[4,128,128]{2,1,0:T(8,128)S(1)}, f32[4,128,128]{2,1,0:T(8,128)S(1)}, u32[]{:S(2)}, u32[]{:S(2)}) collective-permute-start(f32[4,128,128]{2,1,0:T(8,128)S(1)} %get-tuple-element.162), channel_id=1, source_target_pairs={{0,1},{1,2},{2,3},{4,5},{5,6},{6,7},{8,9},{9,10},{10,11},{12,13},{... | collective-permute-start | bytes 786440 | tf_op jit(solution)/shard_map/while/body/eval_jaxpr/ppermute | solution.py:12
  50.8 6.8 %collective-permute-done = f32[4,128,128]{2,1,0:T(8,128)S(1)} collective-permute-done((f32[4,128,128]{2,1,0:T(8,128)S(1)}, f32[4,128,128]{2,1,0:T(8,128)S(1)}, u32[]{:S(2)}, u32[]{:S(2)}) %collective-permute-start) | collective-permute-done | bytes 262176 | tf_op jit(solution)/shard_map/while/body/eval_jaxpr/ppermute | solution.py:12
  57.6 0.4 convolution_add_fusion.4
  58.3 2.2 %collective-permute-start = (f32[4,128,128]{2,1,0:T(8,128)S(1)}, f32[4,128,128]{2,1,0:T(8,128)S(1)}, u32[]{:S(2)}, u32[]{:S(2)}) collective-permute-start(f32[4,128,128]{2,1,0:T(8,128)S(1)} %get-tuple-element.162), channel_id=1, source_target_pairs={{0,1},{1,2},{2,3},{4,5},{5,6},{6,7},{8,9},{9,10},{10,11},{12,13},{... | collective-permute-start | bytes 786440 | tf_op jit(solution)/shard_map/while/body/eval_jaxpr/ppermute | solution.py:12
  60.5 6.8 %collective-permute-done = f32[4,128,128]{2,1,0:T(8,128)S(1)} collective-permute-done((f32[4,128,128]{2,1,0:T(8,128)S(1)}, f32[4,128,128]{2,1,0:T(8,128)S(1)}, u32[]{:S(2)}, u32[]{:S(2)}) %collective-permute-start) | collective-permute-done | bytes 262176 | tf_op jit(solution)/shard_map/while/body/eval_jaxpr/ppermute | solution.py:12
  67.4 0.4 convolution_add_fusion.4
  68.0 1.9 %collective-permute-start = (f32[4,128,128]{2,1,0:T(8,128)S(1)}, f32[4,128,128]{2,1,0:T(8,128)S(1)}, u32[]{:S(2)}, u32[]{:S(2)}) collective-permute-start(f32[4,128,128]{2,1,0:T(8,128)S(1)} %get-tuple-element.162), channel_id=1, source_target_pairs={{0,1},{1,2},{2,3},{4,5},{5,6},{6,7},{8,9},{9,10},{10,11},{12,13},{... | collective-permute-start | bytes 786440 | tf_op jit(solution)/shard_map/while/body/eval_jaxpr/ppermute | solution.py:12
  70.0 6.1 %collective-permute-done = f32[4,128,128]{2,1,0:T(8,128)S(1)} collective-permute-done((f32[4,128,128]{2,1,0:T(8,128)S(1)}, f32[4,128,128]{2,1,0:T(8,128)S(1)}, u32[]{:S(2)}, u32[]{:S(2)}) %collective-permute-start) | collective-permute-done | bytes 262176 | tf_op jit(solution)/shard_map/while/body/eval_jaxpr/ppermute | solution.py:12
  76.8 1.6 %multiply_reduce_fusion.1 = (f32[128,4]{0,1:T(4,128)S(1)}, f32[1,128,4,128]{1,3,2,0:T(8,128)S(1)}) fusion(f32[4,128,128]{1,2,0:T(8,128)S(1)} %fusion.29, f32[4,128,128]{2,1,0:T(8,128)S(1)} %convolution_subtract_fusion.2, f32[4,128,128]{2,1,0:T(8,128)} %get-tuple-element.54), kind=kOutput, calls=%fused_computation.42 | convolution fusion | flops 100859392 | bytes 1050624 | tf_op jit(solution)/shard_map/bik,bkv->biv/dot_general | solution.py:134
  78.6 0.7 convert_element_type.83
  79.3 8.5 %all-to-all-start = ((bf16[1,8,16,512]{3,2,0,1:T(8,128)(2,1)}), bf16[1,8,16,512]{3,2,0,1:T(8,128)(2,1)S(1)}, u32[]{:S(2)}, u32[]{:S(2)}) async-start(bf16[1,8,16,512]{3,2,0,1:T(8,128)(2,1)} %bitcast.32), calls=%async_computation | async-start | bytes 262144 | tf_op jit(solution)/shard_map/all_to_all | solution.py:140
  89.6 0.6 fusion.51
  91.0 0.7 custom-call.9
  92.0 1.6 %all-to-all-done = bf16[1,8,16,512]{3,2,0,1:T(8,128)(2,1)S(1)} async-done(((bf16[1,8,16,512]{3,2,0,1:T(8,128)(2,1)}), bf16[1,8,16,512]{3,2,0,1:T(8,128)(2,1)S(1)}, u32[]{:S(2)}, u32[]{:S(2)}) %all-to-all-start) | async-done | bytes 131104 | tf_op jit(solution)/shard_map/all_to_all | solution.py:140
  93.9 0.6 fusion.14
  94.5 0.5 fusion.19
  95.1 0.6 convolution_subtract_fusion
  95.7 0.6 fusion.2
  96.9 9.3 %all_to_all.8 = bf16[8,1,16,512]{3,2,1,0:T(8,128)(2,1)S(1)} all-to-all(bf16[8,1,16,512]{3,2,1,0:T(8,128)(2,1)S(1)} %bitcast.108), channel_id=1, replica_groups=mesh['line'=8,'scan'=4] {'line'}, dimensions={0} | all-to-all | bytes 262144 | tf_op jit(solution)/shard_map/all_to_all | solution.py:163
  106.1 0.7 copy.87
  (82 shorter events, 6.6 us)
Async XLA Ops:
  0.0 1.7 %copy-start.1 = (bf16[1,128,512]{2,1,0:T(8,128)(2,1)S(1)}, bf16[1,128,512]{2,1,0:T(8,128)(2,1)}, u32[]{:S(2)}) copy-start(bf16[1,128,512]{2,1,0:T(8,128)(2,1)} %param.14) | copy-start | bytes 393220
  1.7 0.9 copy-start.2
  1.8 0.9 copy-start.8
  1.8 1.5 %copy-start.7 = (f32[1,128,4]{1,2,0:T(4,128)S(1)}, f32[1,128,4]{1,2,0:T(4,128)}, u32[]{:S(2)}) copy-start(f32[1,128,4]{1,2,0:T(4,128)} %param.17) | copy-start | bytes 6148
  47.7 10.0 %collective-permute-start = (f32[4,128,128]{2,1,0:T(8,128)S(1)}, f32[4,128,128]{2,1,0:T(8,128)S(1)}, u32[]{:S(2)}, u32[]{:S(2)}) collective-permute-start(f32[4,128,128]{2,1,0:T(8,128)S(1)} %get-tuple-element.162), channel_id=1, source_target_pairs={{0,1},{1,2},{2,3},{4,5},{5,6},{6,7},{8,9},{9,10},{10,11},{12,13},{... | collective-permute-start | bytes 786440 | tf_op jit(solution)/shard_map/while/body/eval_jaxpr/ppermute | solution.py:12
  57.6 0.7 copy-start
  58.3 9.0 %collective-permute-start = (f32[4,128,128]{2,1,0:T(8,128)S(1)}, f32[4,128,128]{2,1,0:T(8,128)S(1)}, u32[]{:S(2)}, u32[]{:S(2)}) collective-permute-start(f32[4,128,128]{2,1,0:T(8,128)S(1)} %get-tuple-element.162), channel_id=1, source_target_pairs={{0,1},{1,2},{2,3},{4,5},{5,6},{6,7},{8,9},{9,10},{10,11},{12,13},{... | collective-permute-start | bytes 786440 | tf_op jit(solution)/shard_map/while/body/eval_jaxpr/ppermute | solution.py:12
  67.4 0.7 copy-start
  68.0 8.0 %collective-permute-start = (f32[4,128,128]{2,1,0:T(8,128)S(1)}, f32[4,128,128]{2,1,0:T(8,128)S(1)}, u32[]{:S(2)}, u32[]{:S(2)}) collective-permute-start(f32[4,128,128]{2,1,0:T(8,128)S(1)} %get-tuple-element.162), channel_id=1, source_target_pairs={{0,1},{1,2},{2,3},{4,5},{5,6},{6,7},{8,9},{9,10},{10,11},{12,13},{... | collective-permute-start | bytes 786440 | tf_op jit(solution)/shard_map/while/body/eval_jaxpr/ppermute | solution.py:12
  76.1 0.7 copy-start
  76.7 1.6 %copy-start.9 = (f32[128]{0:T(128)S(1)}, f32[128]{0:T(128)}, u32[]{:S(2)}) copy-start(f32[128]{0:T(128)} %param.18) | copy-start | bytes 1540
  78.3 9.5 %copy-start.3 = (bf16[8,1,16,512]{3,2,1,0:T(8,128)(2,1)S(1)}, bf16[8,1,16,512]{3,2,1,0:T(8,128)(2,1)}, u32[]{:S(2)}) copy-start(bf16[8,1,16,512]{3,2,1,0:T(8,128)(2,1)} %param.20) | copy-start | bytes 393220
  79.3 14.3 %all-to-all-start = ((bf16[1,8,16,512]{3,2,0,1:T(8,128)(2,1)}), bf16[1,8,16,512]{3,2,0,1:T(8,128)(2,1)S(1)}, u32[]{:S(2)}, u32[]{:S(2)}) async-start(bf16[1,8,16,512]{3,2,0,1:T(8,128)(2,1)} %bitcast.32), calls=%async_computation | async-start | bytes 262144 | tf_op jit(solution)/shard_map/all_to_all | solution.py:140
  87.9 0.7 copy-start.5
  88.0 0.8 copy-start.6
  88.0 1.2 %copy-start.4 = (bf16[8,1,16,512]{3,2,1,0:T(8,128)(2,1)S(1)}, bf16[8,1,16,512]{3,2,1,0:T(8,128)(2,1)}, u32[]{:S(2)}) copy-start(bf16[8,1,16,512]{3,2,1,0:T(8,128)(2,1)} %param.19) | copy-start | bytes 393220
  95.6 0.9 copy-start.10
where the time goes:
time: 108 us; the launch traced here: 107 us
  other arithmetic  42.6 us (39%)
  waiting for transfers between devices  21.3 us (20%)
  starting transfers between devices  15.7 us (15%)
  matrix products  10.3 us (10%)
  blocking collectives  9.27 us (9%)
  local copies, waits for them, and re-layouts  7.05 us (7%)
    another operation x3, other arithmetic, block_terms(): solved = jax.scipy.linalg.solve_triangular(system, right_side, lower=True)  40.1 us
    ppermute x3, waiting for transfers between devices, from_behind(): return lax.ppermute(block, axis, route)  19.7 us
    all_to_all x1, blocking collectives, shards(): lax.all_to_all(normed, 'line', split_axis=0, concat_axis=1, tiled=True)  9.27 us
    all_to_all x1, starting transfers between devices, shards(): lax.all_to_all(arranged, 'line', split_axis=1, concat_axis=0, tiled=True)  8.49 us
    ppermute x3, starting transfers between devices, from_behind(): return lax.ppermute(block, axis, route)  7.25 us
  transfers between devices with their start and end apart: 4, of which 4 were waited for; matrix products, arithmetic and copies ran while one was open for 3% of the time, Pallas kernels for 0%

commit v1 on v0

v1 whole, which is shorter than its diff:
```python
import functools

import jax
import jax.numpy as jnp
from jax import lax
from jax.experimental import pallas as pl
from jax.experimental.pallas import tpu as pltpu
from jax.sharding import PartitionSpec as P

F32 = jnp.float32
BF16 = jnp.bfloat16


def dot(a, b):
    return jnp.dot(a, b, preferred_element_type=F32)


def dot_t(a, b):
    return lax.dot_general(a, b, (((1,), (1,)), ((), ())), preferred_element_type=F32)


def split(a):
    high = a.astype(BF16)
    return high, (a - high.astype(F32)).astype(BF16)


def dot_left(a, b):
    high, low = split(a)
    return dot(high, b) + dot(low, b)


def dot_right(a, b):
    high, low = split(b)
    return dot(a, high) + dot(a, low)


def dot_pairs(a, b):
    return dot(a[0], b[0]) + (dot(a[0], b[1]) + dot(a[1], b[0]))


def masks(size, stride):
    row = lax.broadcasted_iota(jnp.int32, (size, size), 0)
    col = lax.broadcasted_iota(jnp.int32, (size, size), 1)
    same = lax.rem(row, stride) == lax.rem(col, stride)
    return row, col, row == col, same & (row >= col), same & (row > col)


def to_row(column, diagonal):
    return jnp.sum(jnp.where(diagonal, column, 0.0), axis=0, keepdims=True)


def inverse(systems, row, col, diagonal, stride, steps):
    unit = jnp.where(diagonal, 1.0, 0.0)
    base = min(16, steps)
    near = (row // (base * stride)) == (col // (base * stride))
    power = [jnp.where(near, m, 0.0) for m in systems]
    total = [unit - m for m in power]
    reach = 2
    while reach < base:
        halves = [split(m) for m in power]
        power = [dot_pairs(m, m) for m in halves]
        total = [t + dot_pairs(split(t), split(m)) for t, m in zip(total, power)]
        reach *= 2
    size = base
    while size < steps:
        wide = size * 2 * stride
        link = ((row // wide) == (col // wide)) & (
            (row // (size * stride)) != (col // (size * stride))
        )
        halves = [split(t) for t in total]
        inner = [
            dot_pairs(split(jnp.where(link, m, 0.0)), t) for m, t in zip(systems, halves)
        ]
        total = [
            t - dot_pairs(h, split(i)) for t, h, i in zip(total, halves, inner)
        ]
        size *= 2
    return total


def prepare(queries, keys, decay, beta, stride):
    size = keys[0].shape[0]
    steps = size // stride
    row, col, diagonal, lower, strict = masks(size, stride)
    cumulative = jnp.dot(
        jnp.where(lower, 1.0, 0.0), decay, precision=lax.Precision.HIGHEST, preferred_element_type=F32
    )
    heads = range(len(keys))
    cums = [cumulative[:, h : h + 1] for h in heads]
    betas = [beta[:, h : h + 1] for h in heads]
    ratios, systems, attends, units = [], [], [], []
    for h in heads:
        gram = dot_t(keys[h], keys[h])
        squares = jnp.where(diagonal, gram, 0.0)
        unit_col = lax.rsqrt(jnp.sum(squares, axis=1, keepdims=True) + 1e-06)
        unit_row = lax.rsqrt(jnp.sum(squares, axis=0, keepdims=True) + 1e-06)
        spread = cums[h] - to_row(cums[h], diagonal)
        ratio = jnp.where(lower, jnp.exp(jnp.where(lower, spread, 0.0)), 0.0) * unit_row
        systems.append(jnp.where(strict, (betas[h] * unit_col) * (ratio * gram), 0.0))
        attends.append(ratio * dot_t(queries[h], keys[h]))
        units.append(unit_col)
    solved = inverse(systems, row, col, diagonal, stride, steps)
    return solved, attends, cums, betas, units, diagonal


def normed(block, gain):
    return block * lax.rsqrt(jnp.mean(block * block, axis=-1, keepdims=True) + 1e-05) * gain


def each(count, body):
    if count <= 8:
        for i in range(count):
            body(i)
    else:
        lax.fori_loop(0, count, lambda i, c: (body(i), c)[1], 0)


def kernel(
    lines,
    scans,
    query_row,
    key_row,
    value_row,
    decay_row,
    beta_row,
    gain_row,
    query_col,
    key_col,
    decay_col,
    beta_col,
    gain_col,
    out,
    arrived,
    leaving,
    transfer,
    offset,
    local,
    asking,
    mixer,
    outgoing,
    incoming,
    returning,
    returned,
    state_send,
    state_recv,
    there_send,
    there_recv,
    back_send,
    back_recv,
):
    me = lax.axis_index("line")
    place = lax.axis_index("scan")
    tokens, features = query_row.shape[1:]
    size = gain_row.shape[1]
    heads = range(features // size)
    total_rows, width = query_col.shape[0], query_col.shape[2]

    barrier = pltpu.get_barrier_semaphore()

    def greet(i):
        pl.semaphore_signal(
            barrier, inc=1, device_id={"line": lax.rem(me + 1 + i, lines)},
            device_id_type=pl.DeviceIdType.MESH,
        )

    each(lines - 1, greet)

    @pl.when(place > 0)
    def _():
        pl.semaphore_signal(
            barrier, inc=1, device_id={"scan": place - 1}, device_id_type=pl.DeviceIdType.MESH
        )

    @pl.when(place < scans - 1)
    def _():
        pl.semaphore_signal(
            barrier, inc=1, device_id={"scan": place + 1}, device_id_type=pl.DeviceIdType.MESH
        )

    def of_head(ref, h):
        return ref[0, :, h * size : (h + 1) * size]

    queries = [of_head(query_row, h) for h in heads]
    keys = [of_head(key_row, h) for h in heads]
    solved, attends, cums, betas, units, diagonal = prepare(
        queries, keys, decay_row[0], beta_row[0], 1
    )
    for h in heads:
        growth = jnp.exp(cums[h])
        last = cums[h][tokens - 1 : tokens, :]
        tail = jnp.exp(last - cums[h]) * units[h]
        updates = dot_left(solved[h] * to_row(betas[h], diagonal), of_head(value_row, h))
        weighted = dot_left(
            solved[h] * to_row(betas[h] * growth * units[h], diagonal), keys[h]
        )
        both = jnp.concatenate([updates, weighted], axis=1)
        seen = dot_pairs(split(attends[h]), split(both))
        key_t = keys[h].astype(F32).T.astype(BF16)
        kept = dot_right(key_t, tail * both)
        offset[h] = kept[:, :size]
        transfer[h] = jnp.where(diagonal, jnp.exp(last), 0.0) - kept[:, size:]
        local[h] = seen[:, :size]
        asking[h] = growth * queries[h].astype(F32) - seen[:, size:]

    pl.semaphore_wait(
        barrier, lines - 1 + jnp.minimum(place, 1) + jnp.minimum(scans - 1 - place, 1)
    )

    def state_copy(h):
        return pltpu.make_async_remote_copy(
            src_ref=leaving.at[h],
            dst_ref=arrived.at[h],
            send_sem=state_send.at[h],
            recv_sem=state_recv.at[h],
            device_id={"scan": lax.rem(place + 1, scans)},
            device_id_type=pl.DeviceIdType.MESH,
        )

    @pl.when(place == 0)
    def _():
        for h in heads:
            leaving[h] = offset[h].astype(BF16)
            if scans > 1:
                state_copy(h).start()
            arrived[h] = jnp.zeros((size, size), BF16)

    def of_head_col(ref, h):
        block = ref[:, 0, :, h * size : (h + 1) * size]
        return block.reshape(total_rows * width, size)

    def column_terms():
        col_solved, col_attends, _, col_betas, _, col_diagonal = prepare(
            [of_head_col(query_col, h) for h in heads],
            [of_head_col(key_col, h) for h in heads],
            decay_col[:, 0].reshape(total_rows * width, -1),
            beta_col[:, 0].reshape(total_rows * width, -1),
            width,
        )
        for h in heads:
            mixer[h] = dot_pairs(
                split(col_attends[h]),
                split(col_solved[h] * to_row(col_betas[h], col_diagonal)),
            )

    column_terms()

    @pl.when(place > 0)
    def _():
        for h in heads:
            state_copy(h).wait_recv()

            @pl.when(place < scans - 1)
            def _():
                leaving[h] = (dot_left(transfer[h], arrived[h]) + offset[h]).astype(BF16)
                state_copy(h).start()

    def swap(source, target, send, recv, h, i, back=False):
        peer = lax.rem(me + 1 + i, lines)
        return pltpu.make_async_remote_copy(
            src_ref=source.at[h, peer],
            dst_ref=target.at[h, me],
            send_sem=send.at[h, i],
            recv_sem=recv.at[h, me],
            device_id={"line": peer},
            device_id_type=pl.DeviceIdType.MESH,
        )

    def receive(source, target, send, recv, h, i):
        peer = lax.rem(me + 1 + i, lines)
        pltpu.make_async_remote_copy(
            src_ref=source.at[h, peer],
            dst_ref=target.at[h, peer],
            send_sem=send.at[h, i],
            recv_sem=recv.at[h, peer],
            device_id={"line": peer},
            device_id_type=pl.DeviceIdType.MESH,
        ).wait_recv()

    there = (outgoing, incoming, there_send, there_recv)
    back = (returning, returned, back_send, back_recv)

    for h in heads:
        row_out = local[h] + dot_left(asking[h], arrived[h])
        values = normed(row_out, gain_row[...]).astype(BF16)
        outgoing[h] = values.reshape(lines, tokens // lines, size)
        each(lines - 1, lambda i: swap(*there, h, i).start())
        incoming[h, me] = outgoing[h, me]

    for h in heads:
        each(lines - 1, lambda i: receive(*there, h, i))
        values = incoming[h].reshape(total_rows * width, size)
        mixed = normed(dot_left(mixer[h], values), gain_col[...]).astype(BF16)
        returning[h] = mixed.reshape(total_rows, width, size)
        each(lines - 1, lambda i: swap(*back, h, i).start())
        returned[h, me] = returning[h, me]

    for h in heads:
        each(lines - 1, lambda i: receive(*back, h, i))
        out[0, :, h * size : (h + 1) * size] = returned[h].reshape(tokens, size)

    for h in heads:
        each(lines - 1, lambda i: swap(*there, h, i).wait_send())
        each(lines - 1, lambda i: swap(*back, h, i).wait_send())

    @pl.when(place < scans - 1)
    def _():
        for h in heads:
            state_copy(h).wait_send()


def shards(*arrays):
    query_row, gain_row, query_col = arrays[0], arrays[5], arrays[6]
    lines, scans = lax.axis_size("line"), lax.axis_size("scan")
    tokens, features = query_row.shape[1:]
    size = gain_row.shape[0]
    heads = features // size
    arrays = list(arrays)
    arrays[5] = arrays[5].reshape(1, size)
    arrays[10] = arrays[10].reshape(1, size)
    square = (heads, size, size)
    rows = (heads, tokens, size)
    swapped = (heads, lines, tokens // lines, size)
    vmem = pl.BlockSpec(memory_space=pltpu.VMEM)
    return pl.pallas_call(
        functools.partial(kernel, lines, scans),
        out_shape=jax.ShapeDtypeStruct(query_row.shape, BF16),
        in_specs=[vmem] * len(arrays),
        out_specs=vmem,
        scratch_shapes=[
            pltpu.VMEM(square, BF16),
            pltpu.VMEM(square, BF16),
            pltpu.VMEM(square, F32),
            pltpu.VMEM(square, F32),
            pltpu.VMEM(rows, F32),
            pltpu.VMEM(rows, F32),
            pltpu.VMEM(rows, F32),
            pltpu.VMEM(swapped, BF16),
            pltpu.VMEM(swapped, BF16),
            pltpu.VMEM(swapped, BF16),
            pltpu.VMEM(swapped, BF16),
            pltpu.SemaphoreType.DMA((heads,)),
            pltpu.SemaphoreType.DMA((heads,)),
            pltpu.SemaphoreType.DMA((heads, lines)),
            pltpu.SemaphoreType.DMA((heads, lines)),
            pltpu.SemaphoreType.DMA((heads, lines)),
            pltpu.SemaphoreType.DMA((heads, lines)),
        ],
        compiler_params=pltpu.CompilerParams(
            collective_id=0, has_side_effects=True, vmem_limit_bytes=32 * 1024 * 1024
        ),
    )(*arrays)


def solution(mesh):
    placed = (
        P("line", "scan", None),
        P("line", "scan", None),
        P("line", "scan", None),
        P("line", "scan", None),
        P("line", "scan", None),
        P(),
        P(None, "scan", "line", None),
        P(None, "scan", "line", None),
        P(None, "scan", "line", None),
        P(None, "scan", "line", None),
        P(),
    )
    return jax.shard_map(
        shards, mesh=mesh, in_specs=placed, out_specs=P("line", "scan", None), check_vma=False
    )
```

time: 108 us -> 31.4 us (0.29)
  the two profiles are of different devices: /device:TPU:5 before, /device:TPU:7 now
where the time goes in v1:
time: 31.4 us; the launch traced here: 31.2 us
  Pallas kernels  25.7 us (82%)
  local copies, waits for them, and re-layouts  5.45 us (17%)
    pallas_call x1, Pallas kernels, shards(): pl.pallas_call(functools.partial(kernel, lines, scans), out_shape=jax.Sha...  25.7 us
    unnamed x27, local copies, waits for them, and re-layouts  5.45 us

profile of v1, /device:TPU:7, one launch (start us, length us, event | category | flops | bytes accessed | tf_op | source)
XLA Modules:
  0.0 31.2 jit_solution(3488503715335526668)
XLA Ops:
  0.0 0.0 copy-start.9
  0.0 0.0 copy-start.10
  0.0 0.0 copy-start.7
  0.0 0.7 %copy-done.9 = f32[1,128,4]{1,2,0:T(4,128)S(1)} copy-done((f32[1,128,4]{1,2,0:T(4,128)S(1)}, f32[1,128,4]{1,2,0:T(4,128)}, u32[]{:S(2)}) %copy-start.9) | copy-done | bytes 2072
  0.7 0.0 copy-start.8
  0.7 0.0 copy-start.1
  0.7 0.1 copy.12.decay_row
  0.8 0.0 copy-done.10
  0.8 0.0 copy-start
  0.8 0.1 copy.13.beta_row
  0.9 0.0 copy-done.7
  0.9 0.1 copy.14.decay_col
  1.1 0.3 %copy-done.8 = f32[8,1,16,4]{2,3,1,0:T(4,128)S(1)} copy-done((f32[8,1,16,4]{2,3,1,0:T(4,128)S(1)}, f32[8,1,16,4]{2,3,1,0:T(4,128)}, u32[]{:S(2)}) %copy-start.8) | copy-done | bytes 2072
  1.4 0.0 copy-start.5
  1.4 0.0 copy-start.6
  1.4 0.1 copy.15.beta_col
  1.5 0.1 copy-done.1
  1.6 0.1 copy-done
  1.7 0.4 %copy-done.5 = f32[128]{0:T(128)S(1)} copy-done((f32[128]{0:T(128)S(1)}, f32[128]{0:T(128)}, u32[]{:S(2)}) %copy-start.5) | copy-done | bytes 536
  2.1 0.0 copy-done.6
  2.1 0.0 copy-start.2
  2.1 0.9 %copy-done.2 = bf16[1,128,512]{2,1,0:T(8,128)(2,1)S(1)} copy-done((bf16[1,128,512]{2,1,0:T(8,128)(2,1)S(1)}, bf16[1,128,512]{2,1,0:T(8,128)(2,1)}, u32[]{:S(2)}) %copy-start.2) | copy-done | bytes 131096
  3.0 0.0 copy-start.3
  3.0 0.9 %copy-done.3 = bf16[8,1,16,512]{3,2,1,0:T(8,128)(2,1)S(1)} copy-done((bf16[8,1,16,512]{3,2,1,0:T(8,128)(2,1)S(1)}, bf16[8,1,16,512]{3,2,1,0:T(8,128)(2,1)}, u32[]{:S(2)}) %copy-start.3) | copy-done | bytes 131096
  3.9 0.0 copy-start.4
  3.9 0.9 %copy-done.4 = bf16[8,1,16,512]{3,2,1,0:T(8,128)(2,1)S(1)} copy-done((bf16[8,1,16,512]{3,2,1,0:T(8,128)(2,1)S(1)}, bf16[8,1,16,512]{3,2,1,0:T(8,128)(2,1)}, u32[]{:S(2)}) %copy-start.4) | copy-done | bytes 131096
  4.8 25.7 %shard_map.109 = bf16[1,128,512]{2,1,0:T(8,128)(2,1)S(1)} custom-call(bf16[1,128,512]{2,1,0:T(8,128)(2,1)S(1)} %copy-done, bf16[1,128,512]{2,1,0:T(8,128)(2,1)S(1)} %copy-done.1, bf16[1,128,512]{2,1,0:T(8,128)(2,1)S(1)} %copy-done.2, f32[1,128,4]{2,1,0:T(8,128)S(1)} %copy.12.decay_row, f32[1,128,4]{2,1,0:T(8,128)S(1)} %copy.13.beta_row, ...), custom_call_target="tpu_custom_call" | custom-call | tf_op jit(solution)/shard_map/pallas_call | solution.py:324
  30.6 0.7 %copy.17 = bf16[1,128,512]{2,1,0:T(8,128)(2,1)} copy(bf16[1,128,512]{2,1,0:T(8,128)(2,1)S(1)} %shard_map.109) | data formatting | bytes 262144
Async XLA Ops:
  0.0 0.7 %copy-start.9 = (f32[1,128,4]{1,2,0:T(4,128)S(1)}, f32[1,128,4]{1,2,0:T(4,128)}, u32[]{:S(2)}) copy-start(f32[1,128,4]{1,2,0:T(4,128)} %param.14) | copy-start | bytes 6148
  0.0 0.8 %copy-start.10 = (f32[1,128,4]{1,2,0:T(4,128)S(1)}, f32[1,128,4]{1,2,0:T(4,128)}, u32[]{:S(2)}) copy-start(f32[1,128,4]{1,2,0:T(4,128)} %param.15) | copy-start | bytes 6148
  0.0 0.9 %copy-start.7 = (f32[8,1,16,4]{2,3,1,0:T(4,128)S(1)}, f32[8,1,16,4]{2,3,1,0:T(4,128)}, u32[]{:S(2)}) copy-start(f32[8,1,16,4]{2,3,1,0:T(4,128)} %param.19) | copy-start | bytes 6148
  0.7 0.7 %copy-start.8 = (f32[8,1,16,4]{2,3,1,0:T(4,128)S(1)}, f32[8,1,16,4]{2,3,1,0:T(4,128)}, u32[]{:S(2)}) copy-start(f32[8,1,16,4]{2,3,1,0:T(4,128)} %param.20) | copy-start | bytes 6148
  0.7 0.9 %copy-start.1 = (bf16[1,128,512]{2,1,0:T(8,128)(2,1)S(1)}, bf16[1,128,512]{2,1,0:T(8,128)(2,1)}, u32[]{:S(2)}) copy-start(bf16[1,128,512]{2,1,0:T(8,128)(2,1)} %key_row.1) | copy-start | bytes 393220
  0.8 0.9 %copy-start = (bf16[1,128,512]{2,1,0:T(8,128)(2,1)S(1)}, bf16[1,128,512]{2,1,0:T(8,128)(2,1)}, u32[]{:S(2)}) copy-start(bf16[1,128,512]{2,1,0:T(8,128)(2,1)} %query_row.1) | copy-start | bytes 393220
  1.4 0.7 %copy-start.5 = (f32[128]{0:T(128)S(1)}, f32[128]{0:T(128)}, u32[]{:S(2)}) copy-start(f32[128]{0:T(128)} %param.16) | copy-start | bytes 1540
  1.4 0.7 %copy-start.6 = (f32[128]{0:T(128)S(1)}, f32[128]{0:T(128)}, u32[]{:S(2)}) copy-start(f32[128]{0:T(128)} %param.21) | copy-start | bytes 1540
  2.1 0.9 %copy-start.2 = (bf16[1,128,512]{2,1,0:T(8,128)(2,1)S(1)}, bf16[1,128,512]{2,1,0:T(8,128)(2,1)}, u32[]{:S(2)}) copy-start(bf16[1,128,512]{2,1,0:T(8,128)(2,1)} %value_row.1) | copy-start | bytes 393220
  3.0 0.9 %copy-start.3 = (bf16[8,1,16,512]{3,2,1,0:T(8,128)(2,1)S(1)}, bf16[8,1,16,512]{3,2,1,0:T(8,128)(2,1)}, u32[]{:S(2)}) copy-start(bf16[8,1,16,512]{3,2,1,0:T(8,128)(2,1)} %query_col.1) | copy-start | bytes 393220
  3.9 0.9 %copy-start.4 = (bf16[8,1,16,512]{3,2,1,0:T(8,128)(2,1)S(1)}, bf16[8,1,16,512]{3,2,1,0:T(8,128)(2,1)}, u32[]{:S(2)}) copy-start(bf16[8,1,16,512]{3,2,1,0:T(8,128)(2,1)} %key_col.1) | copy-start | bytes 393220

commit v2 on v1

--- a/solution.py
+++ b/solution.py
@@ -118,73 +118,95 @@
 def kernel(
     lines,
     scans,
-    query_row,
-    key_row,
-    value_row,
-    decay_row,
-    beta_row,
-    gain_row,
-    query_col,
-    key_col,
-    decay_col,
-    beta_col,
-    gain_col,
-    out,
-    arrived,
-    leaving,
-    transfer,
-    offset,
-    local,
-    asking,
-    mixer,
-    outgoing,
-    incoming,
-    returning,
-    returned,
-    state_send,
-    state_recv,
-    there_send,
-    there_recv,
-    back_send,
-    back_recv,
+    *refs,
 ):
+    hbm, out, held = refs[:11], refs[11], refs[12:23]
+    (
+        state,
+        own,
+        gift_out,
+        gift_in,
+        chain_out,
+        chain_in,
+        transfer,
+        offset,
+        local,
+        asking,
+        mixer,
+        outgoing,
+        incoming,
+        returning,
+        returned,
+        load_sem,
+        gift_send,
+        gift_recv,
+        chain_send,
+        chain_recv,
+        there_send,
+        there_recv,
+        back_send,
+        back_recv,
+    ) = refs[23:]
+    (
+        query_row,
+        key_row,
+        value_row,
+        decay_row,
+        beta_row,
+        gain_row,
+        query_col,
+        key_col,
+        decay_col,
+        beta_col,
+        gain_col,
+    ) = held
     me = lax.axis_index("line")
     place = lax.axis_index("scan")
+    odd = lax.rem(place, 2)
     tokens, features = query_row.shape[1:]
     size = gain_row.shape[1]
     heads = range(features // size)
     total_rows, width = query_col.shape[0], query_col.shape[2]
+    groups = outgoing.shape[0]
+    group_heads = outgoing.shape[2]
+    mesh_id = pl.DeviceIdType.MESH
+
+    def load(i):
+        return pltpu.make_async_copy(hbm[i], held[i], load_sem.at[i])
+
+    for i in (1, 3, 4, 0, 2, 5, 7, 6, 8, 9, 10):
+        load(i).start()
 
     barrier = pltpu.get_barrier_semaphore()
 
     def greet(i):
         pl.semaphore_signal(
-            barrier, inc=1, device_id={"line": lax.rem(me + 1 + i, lines)},
-            device_id_type=pl.DeviceIdType.MESH,
+            barrier, inc=1, device_id={"line": lax.rem(me + 1 + i, lines)}, device_id_type=mesh_id
         )
 
     each(lines - 1, greet)
 
-    @pl.when(place > 0)
-    def _():
+    def greet_along(distance):
         pl.semaphore_signal(
-            barrier, inc=1, device_id={"scan": place - 1}, device_id_type=pl.DeviceIdType.MESH
-        )
-
-    @pl.when(place < scans - 1)
-    def _():
-        pl.semaphore_signal(
-            barrier, inc=1, device_id={"scan": place + 1}, device_id_type=pl.DeviceIdType.MESH
-        )
+            barrier, inc=1, device_id={"scan": place + distance}, device_id_type=mesh_id
+        )
+
+    pl.when(place > 0)(lambda: greet_along(-1))
+    pl.when(place < scans - 1)(lambda: greet_along(1))
+    pl.when((odd == 1) & (place > 1))(lambda: greet_along(-2))
+    pl.when((odd == 1) & (place < scans - 2))(lambda: greet_along(2))
 
     def of_head(ref, h):
         return ref[0, :, h * size : (h + 1) * size]
 
+    for i in (1, 3, 4, 0):
+        load(i).wait()
     queries = [of_head(query_row, h) for h in heads]
     keys = [of_head(key_row, h) for h in heads]
     solved, attends, cums, betas, units, diagonal = prepare(
         queries, keys, decay_row[0], beta_row[0], 1
     )
+    load(2).wait()
     for h in heads:
         growth = jnp.exp(cums[h])
         last = cums[h][tokens - 1 : tokens, :]
@@ -194,35 +216,61 @@
             solved[h] * to_row(betas[h] * growth * units[h], diagonal), keys[h]
         )
         both = jnp.concatenate([updates, weighted], axis=1)
-        seen = dot_pairs(split(attends[h]), split(both))
+        own[h] = both
         key_t = keys[h].astype(F32).T.astype(BF16)
         kept = dot_right(key_t, tail * both)
         offset[h] = kept[:, :size]
         transfer[h] = jnp.where(diagonal, jnp.exp(last), 0.0) - kept[:, size:]
+
+    pl.semaphore_wait(
+        barrier,
+        lines
+        - 1
+        + jnp.minimum(place, 1)
+        + jnp.minimum(scans - 1 - place, 1)
+        + odd * (jnp.minimum(place // 2, 1) + jnp.minimum((scans - 1 - place) // 2, 1)),
+    )
+
+    def gift(which, h):
+        return pltpu.make_async_remote_copy(
+            src_ref=gift_out.at[which, h],
+            dst_ref=gift_in.at[which, h],
+            send_sem=gift_send.at[which, h],
+            recv_sem=gift_recv.at[which, h],
+            device_id={"scan": lax.rem(place + 1, scans)},
+            device_id_type=mesh_id,
+        )
+
+    def chain(h, distance):
+        return pltpu.make_async_remote_copy(
+            src_ref=chain_out.at[h],
+            dst_ref=chain_in.at[h],
+            send_sem=chain_send.at[distance - 1, h],
+            recv_sem=chain_recv.at[h],
+            device_id={"scan": lax.rem(place + distance, scans)},
+            device_id_type=mesh_id,
+        )
+
+    gives = (odd == 0) & (place < scans - 1)
+
+    @pl.when(gives)
+    def _():
+        for h in heads:
+            gift_out[0, h] = offset[h].astype(BF16)
+            gift(0, h).start()
+
+            @pl.when(place > 0)
+            def _():
+                gift_out[1, h] = transfer[h].astype(BF16)
+                gift(1, h).start()
+
+    for h in heads:
+        seen = dot_pairs(split(attends[h]), split(own[h]))
         local[h] = seen[:, :size]
-        asking[h] = growth * queries[h].astype(F32) - seen[:, size:]
-
-    pl.semaphore_wait(
-        barrier, lines - 1 + jnp.minimum(place, 1) + jnp.minimum(scans - 1 - place, 1)
-    )
-
-    def state_copy(h):
-        return pltpu.make_async_remote_copy(
-            src_ref=leaving.at[h],
-            dst_ref=arrived.at[h],
-            send_sem=state_send.at[h],
-            recv_sem=state_recv.at[h],
-            device_id={"scan": lax.rem(place + 1, scans)},
-            device_id_type=pl.DeviceIdType.MESH,
-        )
-
-    @pl.when(place == 0)
-    def _():
-        for h in heads:
-            leaving[h] = offset[h].astype(BF16)
-            if scans > 1:
-                state_copy(h).start()
-            arrived[h] = jnp.zeros((size, size), BF16)
+        asking[h] = jnp.exp(cums[h]) * queries[h].astype(F32) - seen[:, size:]
+
+    for i in (5, 7, 6, 8, 9, 10):
+        load(i).wait()
 
     def of_head_col(ref, h):
         block = ref[:, 0, :, h * size : (h + 1) * size]
@@ -242,91 +290,135 @@
                 split(col_solved[h] * to_row(col_betas[h], col_diagonal)),
             )
 
-    column_terms()
-
-    @pl.when(place > 0)
-    def _():
-        for h in heads:
-            state_copy(h).wait_recv()
+    pl.when(place >= 2)(column_terms)
+
+    @pl.when(place == 0)
+    def _():
+        state[...] = jnp.zeros_like(state)
+
+    @pl.when(odd == 1)
+    def _():
+        for h in heads:
+            gift(0, h).wait_recv()
+
+            @pl.when(place == 1)
+            def _():
+                state[h] = gift_in[0, h]
+
+            @pl.when(place > 1)
+            def _():
+                gift(1, h).wait_recv()
+                chain(h, 1).wait_recv()
+                state[h] = (
+                    dot(gift_in[1, h], chain_in[h]) + gift_in[0, h].astype(F32)
+                ).astype(BF16)
 
             @pl.when(place < scans - 1)
             def _():
-                leaving[h] = (dot_left(transfer[h], arrived[h]) + offset[h]).astype(BF16)
-                state_copy(h).start()
-
-    def swap(source, target, send, recv, h, i, back=False):
+                chain_out[h] = (dot_left(transfer[h], state[h]) + offset[h]).astype(BF16)
+                chain(h, 1).start()
+                pl.when(place < scans - 2)(lambda: chain(h, 2).start())
+
+    @pl.when((odd == 0) & (place > 0))
+    def _():
+        for h in heads:
+            chain(h, 1).wait_recv()
+            state[h] = chain_in[h]
+
+    def swap(source, target, send, recv, g, i):
         peer = lax.rem(me + 1 + i, lines)
         return pltpu.make_async_remote_copy(
-            src_ref=source.at[h, peer],
-            dst_ref=target.at[h, me],
-            send_sem=send.at[h, i],
-            recv_sem=recv.at[h, me],
+            src_ref=source.at[g, peer],
+            dst_ref=target.at[g, me],
+            send_sem=send.at[g, i],
+            recv_sem=recv.at[g, me],
             device_id={"line": peer},
-            device_id_type=pl.DeviceIdType.MESH,
-        )
-
-    def receive(source, target, send, recv, h, i):
+            device_id_type=mesh_id,
+        )
+
+    def receive(source, target, send, recv, g, i):
         peer = lax.rem(me + 1 + i, lines)
         pltpu.make_async_remote_copy(
-            src_ref=source.at[h, peer],
-            dst_ref=target.at[h, peer],
-            send_sem=send.at[h, i],
-            recv_sem=recv.at[h, peer],
+            src_ref=source.at[g, peer],
+            dst_ref=target.at[g, peer],
+            send_sem=send.at[g, i],
+            recv_sem=recv.at[g, peer],
             device_id={"line": peer},
-            device_id_type=pl.DeviceIdType.MESH,
+            device_id_type=mesh_id,
         ).wait_recv()
 
     there = (outgoing, incoming, there_send, there_recv)
     back = (returning, returned, back_send, back_recv)
 
-    for h in heads:
-        row_out = local[h] + dot_left(asking[h], arrived[h])
-        values = normed(row_out, gain_row[...]).astype(BF16)
-        outgoing[h] = values.reshape(lines, tokens // lines, size)
-        each(lines - 1, lambda i: swap(*there, h, i).start())
-        incoming[h, me] = outgoing[h, me]
-
-    for h in heads:
-        each(lines - 1, lambda i: receive(*there, h, i))
-        values = incoming[h].reshape(total_rows * width, size)
-        mixed = normed(dot_left(mixer[h], values), gain_col[...]).astype(BF16)
-        returning[h] = mixed.reshape(total_rows, width, size)
-        each(lines - 1, lambda i: swap(*back, h, i).start())
-        returned[h, me] = returning[h, me]
-
-    for h in heads:
-        each(lines - 1, lambda i: receive(*back, h, i))
-        out[0, :, h * size : (h + 1) * size] = returned[h].reshape(tokens, size)
-
-    for h in heads:
-        each(lines - 1, lambda i: swap(*there, h, i).wait_send())
-        each(lines - 1, lambda i: swap(*back, h, i).wait_send())
-
-    @pl.when(place < scans - 1)
-    def _():
-        for h in heads:
-            state_copy(h).wait_send()
+    for g in range(groups):
+        for j in range(group_heads):
+            h = g * group_heads + j
+            row_out = local[h] + dot_left(asking[h], state[h])
+            values = normed(row_out, gain_row[...]).astype(BF16)
+            outgoing[g, :, j] = values.reshape(lines, tokens // lines, size)
+        each(lines - 1, lambda i: swap(*there, g, i).start())
+        incoming[g, me] = outgoing[g, me]
+
+    pl.when(place < 2)(column_terms)
+
+    for g in range(groups):
+        each(lines - 1, lambda i: receive(*there, g, i))
+        for j in range(group_heads):
+            h = g * group_heads + j
+            values = incoming[g, :, j].reshape(total_rows * width, size)
+            mixed = normed(dot_left(mixer[h], values), gain_col[...]).astype(BF16)
+            returning[g, :, j] = mixed.reshape(total_rows, width, size)
+        each(lines - 1, lambda i: swap(*back, g, i).start())
+        returned[g, me] = returning[g, me]
+
+    for g in range(groups):
+        each(lines - 1, lambda i: receive(*back, g, i))
+        for j in range(group_heads):
+            h = g * group_heads + j
+            out[0, :, h * size : (h + 1) * size] = returned[g, :, j].reshape(tokens, size)
+
+    for g in range(groups):
+        each(lines - 1, lambda i: swap(*there, g, i).wait_send())
+        each(lines - 1, lambda i: swap(*back, g, i).wait_send())
+
+    @pl.when(gives)
+    def _():
+        for h in heads:
+            gift(0, h).wait_send()
+            pl.when(place > 0)(lambda: gift(1, h).wait_send())
+
+    @pl.when((odd == 1) & (place < scans - 1))
+    def _():
+        for h in heads:
+            chain(h, 1).wait_send()
+            pl.when(place < scans - 2)(lambda: chain(h, 2).wait_send())
 
 
 def shards(*arrays):
-    query_row, gain_row, query_col = arrays[0], arrays[5], arrays[6]
+    query_row, gain_row = arrays[0], arrays[5]
     lines, scans = lax.axis_size("line"), lax.axis_size("scan")
     tokens, features = query_row.shape[1:]
     size = gain_row.shape[0]
     heads = features // size
+    groups = 2 if heads % 2 == 0 else 1
     arrays = list(arrays)
     arrays[5] = arrays[5].reshape(1, size)
     arrays[10] = arrays[10].reshape(1, size)
     square = (heads, size, size)
     rows = (heads, tokens, size)
-    swapped = (heads, lines, tokens // lines, size)
-    vmem = pl.BlockSpec(memory_space=pltpu.VMEM)
+    swapped = (groups, lines, heads // groups, tokens // lines, size)
+    dma = pltpu.SemaphoreType.DMA
     return pl.pallas_call(
         functools.partial(kernel, lines, scans),
         out_shape=jax.ShapeDtypeStruct(query_row.shape, BF16),
-        in_specs=[vmem] * len(arrays),
-        out_specs=vmem,
-        scratch_shapes=[
+        in_specs=[pl.BlockSpec(memory_space=pl.ANY)] * len(arrays),
+        out_specs=pl.BlockSpec(memory_space=pltpu.VMEM),
+        scratch_shapes=[pltpu.VMEM(a.shape, a.dtype) for a in arrays]
+        + [
+            pltpu.VMEM(square, BF16),
+            pltpu.VMEM((heads, tokens, 2 * size), F32),
+            pltpu.VMEM((2,) + square, BF16),
+            pltpu.VMEM((2,) + square, BF16),
             pltpu.VMEM(square, BF16),
             pltpu.VMEM(square, BF16),
             pltpu.VMEM(square, F32),
@@ -338,15 +430,18 @@
             pltpu.VMEM(swapped, BF16),
             pltpu.VMEM(swapped, BF16),
             pltpu.VMEM(swapped, BF16),
-            pltpu.SemaphoreType.DMA((heads,)),
-            pltpu.SemaphoreType.DMA((heads,)),
-            pltpu.SemaphoreType.DMA((heads, lines)),
-            pltpu.SemaphoreType.DMA((heads, lines)),
-            pltpu.SemaphoreType.DMA((heads, lines)),
-            pltpu.SemaphoreType.DMA((heads, lines)),
+            dma((len(arrays),)),
+            dma((2, heads)),
+            dma((2, heads)),
+            dma((2, heads)),
+            dma((heads,)),
+            dma((groups, lines)),
+            dma((groups, lines)),
+            dma((groups, lines)),
+            dma((groups, lines)),
         ],
         compiler_params=pltpu.CompilerParams(
-            collective_id=0, has_side_effects=True, vmem_limit_bytes=32 * 1024 * 1024
+            collective_id=0, has_side_effects=True, vmem_limit_bytes=56 * 1024 * 1024
         ),
     )(*arrays)
 

time: 31.4 us -> 29.6 us (0.943)
  the two profiles are of different devices: /device:TPU:7 before, /device:TPU:5 now
where the time goes in v2:
time: 29.6 us; the launch traced here: 29.3 us
  Pallas kernels  24 us (81%)
  local copies, waits for them, and re-layouts  5.22 us (18%)
    pallas_call x1, Pallas kernels, shards(): pl.pallas_call(functools.partial(kernel, lines, scans), out_shape=jax.Sha...  24 us
    unnamed x13, local copies, waits for them, and re-layouts  5.22 us

profile of v2, /device:TPU:5, one launch (start us, length us, event | category | flops | bytes accessed | tf_op | source)
XLA Modules:
  0.0 29.3 jit_solution(11559265812965415175)
XLA Ops:
  0.0 0.0 copy-start.2
  0.0 0.7 %copy-done.2 = f32[1,128,4]{1,2,0:T(4,128)S(1)} copy-done((f32[1,128,4]{1,2,0:T(4,128)S(1)}, f32[1,128,4]{1,2,0:T(4,128)}, u32[]{:S(2)}) %copy-start.2) | copy-done | bytes 2072
  0.7 0.0 copy-start.3
  0.7 0.7 %copy.12.refs_3_ = f32[1,128,4]{2,1,0:T(8,128)} copy(f32[1,128,4]{1,2,0:T(4,128)S(1)} %copy-done.2) | data formatting | bytes 4096 | tf_op args[3]
  1.4 0.0 copy-done.3
  1.4 0.0 copy-start
  1.4 0.7 %copy.13.refs_4_ = f32[1,128,4]{2,1,0:T(8,128)} copy(f32[1,128,4]{1,2,0:T(4,128)S(1)} %copy-done.3) | data formatting | bytes 4096 | tf_op args[4]
  2.2 0.0 copy-done
  2.2 0.0 copy-start.1
  2.2 0.7 %copy.14.refs_8_ = f32[8,1,16,4]{3,2,1,0:T(8,128)} copy(f32[8,1,16,4]{2,3,1,0:T(4,128)S(1)} %copy-done) | data formatting | bytes 4096 | tf_op args[8]
  2.9 0.0 copy-done.1
  2.9 0.8 %copy.15.refs_9_ = f32[8,1,16,4]{3,2,1,0:T(8,128)} copy(f32[8,1,16,4]{2,3,1,0:T(4,128)S(1)} %copy-done.1) | data formatting | bytes 4096 | tf_op args[9]
  3.7 24.0 %shard_map.109 = bf16[1,128,512]{2,1,0:T(8,128)(2,1)} custom-call(bf16[1,128,512]{2,1,0:T(8,128)(2,1)} %refs_0_.1, bf16[1,128,512]{2,1,0:T(8,128)(2,1)} %refs_1_.1, bf16[1,128,512]{2,1,0:T(8,128)(2,1)} %refs_2_.1, f32[1,128,4]{2,1,0:T(8,128)} %copy.12.refs_3_, f32[1,128,4]{2,1,0:T(8,128)} %copy.13.refs_4_, f32[1,128]{1,0:T(1,128)} %bitcast.2, ...), custom_call_target="tpu_custom_call" | custom-call | tf_op jit(solution)/shard_map/pallas_call | solution.py:411
  27.7 1.6 %copy.17 = bf16[1,128,512]{2,1,0:T(8,128)(2,1)} copy(bf16[1,128,512]{2,1,0:T(8,128)(2,1)} %shard_map.109) | data formatting | bytes 262144
Async XLA Ops:
  0.0 0.7 %copy-start.2 = (f32[1,128,4]{1,2,0:T(4,128)S(1)}, f32[1,128,4]{1,2,0:T(4,128)}, u32[]{:S(2)}) copy-start(f32[1,128,4]{1,2,0:T(4,128)} %param.14) | copy-start | bytes 6148
  0.7 0.7 %copy-start.3 = (f32[1,128,4]{1,2,0:T(4,128)S(1)}, f32[1,128,4]{1,2,0:T(4,128)}, u32[]{:S(2)}) copy-start(f32[1,128,4]{1,2,0:T(4,128)} %param.15) | copy-start | bytes 6148
  1.4 0.7 %copy-start = (f32[8,1,16,4]{2,3,1,0:T(4,128)S(1)}, f32[8,1,16,4]{2,3,1,0:T(4,128)}, u32[]{:S(2)}) copy-start(f32[8,1,16,4]{2,3,1,0:T(4,128)} %param.19) | copy-start | bytes 6148
  2.2 0.7 %copy-start.1 = (f32[8,1,16,4]{2,3,1,0:T(4,128)S(1)}, f32[8,1,16,4]{2,3,1,0:T(4,128)}, u32[]{:S(2)}) copy-start(f32[8,1,16,4]{2,3,1,0:T(4,128)} %param.20) | copy-start | bytes 6148

commit v3 on v2

v3 whole, which is shorter than its diff:
```python
import functools

import jax
import jax.numpy as jnp
from jax import lax
from jax.experimental import pallas as pl
from jax.experimental.pallas import tpu as pltpu
from jax.sharding import PartitionSpec as P

F32 = jnp.float32
BF16 = jnp.bfloat16


def dot(a, b):
    return jnp.dot(a, b, preferred_element_type=F32)


def dot_t(a, b):
    return lax.dot_general(a, b, (((1,), (1,)), ((), ())), preferred_element_type=F32)


def split(a):
    high = a.astype(BF16)
    return high, (a - high.astype(F32)).astype(BF16)


def dot_left(a, b):
    high, low = split(a)
    return dot(high, b) + dot(low, b)


def dot_right(a, b):
    high, low = split(b)
    return dot(a, high) + dot(a, low)


def dot_pairs(a, b):
    return dot(a[0], b[0]) + (dot(a[0], b[1]) + dot(a[1], b[0]))


def masks(size, stride):
    row = lax.broadcasted_iota(jnp.int32, (size, size), 0)
    col = lax.broadcasted_iota(jnp.int32, (size, size), 1)
    same = lax.rem(row, stride) == lax.rem(col, stride)
    return row, col, row == col, same & (row >= col), same & (row > col)


def to_row(column, diagonal):
    return jnp.sum(jnp.where(diagonal, column, 0.0), axis=0, keepdims=True)


def dot16(a, b):
    return dot(a.astype(BF16), b.astype(BF16))


def inverse(systems, row, col, diagonal, stride, steps, refine):
    unit = jnp.where(diagonal, 1.0, 0.0)
    base = min(16, steps)
    near = (row // (base * stride)) == (col // (base * stride))
    power = [jnp.where(near, m, 0.0) for m in systems]
    total = [unit - m for m in power]
    reach = 2
    while reach < base:
        power = [dot16(m, m) for m in power]
        total = [t + dot16(t, m) for t, m in zip(total, power)]
        reach *= 2
    size = base
    while size < steps:
        wide = size * 2 * stride
        link = ((row // wide) == (col // wide)) & (
            (row // (size * stride)) != (col // (size * stride))
        )
        inner = [dot16(jnp.where(link, m, 0.0), t) for m, t in zip(systems, total)]
        total = [t - dot16(t, i) for t, i in zip(total, inner)]
        size *= 2
    if refine:
        left = [
            (unit - t) - dot_pairs(split(m), split(t)) for m, t in zip(systems, total)
        ]
        total = [t + dot16(t, e) for t, e in zip(total, left)]
    return total


def prepare(queries, keys, decay, beta, stride, refine):
    size = keys[0].shape[0]
    steps = size // stride
    count = len(keys)
    row, col, diagonal, lower, strict = masks(size, stride)
    rest, cumulative = decay, 0.0
    upper = jnp.where(
        (lax.rem(row, stride) == lax.rem(col, stride)) & (row <= col), 1.0, 0.0
    ).astype(BF16)
    for _ in range(3):
        piece = rest.astype(BF16)
        rest = rest - piece.astype(F32)
        cumulative = cumulative + dot(piece, upper)
    packed = jnp.concatenate([cumulative, beta], axis=0).T
    cum_rows = [cumulative[h : h + 1] for h in range(count)]
    beta_rows = [beta[h : h + 1] for h in range(count)]
    cums = [packed[:, h : h + 1] for h in range(count)]
    systems, attends, units, unit_rows = [], [], [], []
    for h in range(count):
        gram = dot_t(keys[h], keys[h])
        squares = jnp.where(diagonal, gram, 0.0)
        unit_col = lax.rsqrt(jnp.sum(squares, axis=1, keepdims=True) + 1e-06)
        unit_row = lax.rsqrt(jnp.sum(squares, axis=0, keepdims=True) + 1e-06)
        spread = cums[h] - cum_rows[h]
        ratio = jnp.where(lower, jnp.exp(jnp.where(lower, spread, 0.0)), 0.0) * unit_row
        beta_col = packed[:, count + h : count + h + 1]
        systems.append(jnp.where(strict, (beta_col * unit_col) * (ratio * gram), 0.0))
        attends.append(ratio * dot_t(queries[h], keys[h]))
        units.append(unit_col)
        unit_rows.append(unit_row)
    solved = inverse(systems, row, col, diagonal, stride, steps, refine)
    return solved, attends, cums, units, cum_rows, beta_rows, unit_rows, diagonal


def normed(block, gain):
    return block * lax.rsqrt(jnp.mean(block * block, axis=-1, keepdims=True) + 1e-05) * gain


def each(count, body):
    if count <= 8:
        for i in range(count):
            body(i)
    else:
        lax.fori_loop(0, count, lambda i, c: (body(i), c)[1], 0)


def kernel(
    lines,
    scans,
    *refs,
):
    hbm, out, held = refs[:11], refs[11], refs[12:23]
    (
        state,
        gift_out,
        gift_in,
        chain_out,
        chain_in,
        offset,
        local,
        asking,
        mixer,
        outgoing,
        incoming,
        returning,
        returned,
        load_sem,
        gift_send,
        gift_recv,
        chain_send,
        chain_recv,
        there_send,
        there_recv,
        back_send,
        back_recv,
    ) = refs[23:]
    (
        query_row,
        key_row,
        value_row,
        decay_row,
        beta_row,
        gain_row,
        query_col,
        key_col,
        decay_col,
        beta_col,
        gain_col,
    ) = held
    me = lax.axis_index("line")
    place = lax.axis_index("scan")
    odd = lax.rem(place, 2)
    tokens, features = query_row.shape[1:]
    size = gain_row.shape[1]
    heads = range(features // size)
    total_rows, width = query_col.shape[0], query_col.shape[2]
    groups = outgoing.shape[0]
    group_heads = outgoing.shape[2]
    mesh_id = pl.DeviceIdType.MESH

    def load(i):
        return pltpu.make_async_copy(hbm[i], held[i], load_sem.at[i])

    for i in (1, 3, 4, 0, 2, 5, 7, 6, 8, 9, 10):
        load(i).start()

    barrier = pltpu.get_barrier_semaphore()

    def greet(i):
        pl.semaphore_signal(
            barrier, inc=1, device_id={"line": lax.rem(me + 1 + i, lines)}, device_id_type=mesh_id
        )

    each(lines - 1, greet)

    def greet_along(distance):
        pl.semaphore_signal(
            barrier, inc=1, device_id={"scan": place + distance}, device_id_type=mesh_id
        )

    pl.when(place > 0)(lambda: greet_along(-1))
    pl.when(place < scans - 1)(lambda: greet_along(1))
    pl.when((odd == 1) & (place > 1))(lambda: greet_along(-2))
    pl.when((odd == 1) & (place < scans - 2))(lambda: greet_along(2))

    def of_head(ref, h):
        return ref[0, :, h * size : (h + 1) * size]

    for i in (1, 3, 4, 0):
        load(i).wait()
    queries = [of_head(query_row, h) for h in heads]
    keys = [of_head(key_row, h) for h in heads]
    solved, attends, cums, units, cum_rows, beta_rows, unit_rows, diagonal = prepare(
        queries, keys, decay_row[0], beta_row[0], 1, True
    )
    load(2).wait()
    pl.semaphore_wait(
        barrier,
        lines
        - 1
        + jnp.minimum(place, 1)
        + jnp.minimum(scans - 1 - place, 1)
        + odd * (jnp.minimum(place // 2, 1) + jnp.minimum((scans - 1 - place) // 2, 1)),
    )

    def gift(which, g):
        return pltpu.make_async_remote_copy(
            src_ref=gift_out.at[which, g],
            dst_ref=gift_in.at[which, g],
            send_sem=gift_send.at[which, g],
            recv_sem=gift_recv.at[which, g],
            device_id={"scan": lax.rem(place + 1, scans)},
            device_id_type=mesh_id,
        )

    def chain(g, distance):
        return pltpu.make_async_remote_copy(
            src_ref=chain_out.at[g],
            dst_ref=chain_in.at[g],
            send_sem=chain_send.at[distance - 1, g],
            recv_sem=chain_recv.at[g],
            device_id={"scan": lax.rem(place + distance, scans)},
            device_id_type=mesh_id,
        )

    gives = (odd == 0) & (place < scans - 1)
    lasts = [c[tokens - 1 : tokens, :] for c in cums]
    tails = [jnp.exp(lasts[h] - cums[h]) * units[h] for h in heads]
    keys_t = [k.astype(F32).T.astype(BF16) for k in keys]
    updates, weighted = {}, {}
    for g in range(groups):
        for j in range(group_heads):
            h = g * group_heads + j
            updates[h] = dot_left(solved[h] * beta_rows[h], of_head(value_row, h))
            offset[h] = dot(keys_t[h], (tails[h] * updates[h]).astype(BF16))
            gift_out[0, g, j] = offset[h].astype(BF16)
        pl.when(gives)(lambda: gift(0, g).start())
    for h in heads:
        weighted[h] = dot_left(
            solved[h] * (beta_rows[h] * jnp.exp(cum_rows[h]) * unit_rows[h]), keys[h]
        )
        kept = dot(keys_t[h], (tails[h] * weighted[h]).astype(BF16))
        gift_out[1, h // group_heads, h % group_heads] = (
            jnp.where(diagonal, jnp.exp(lasts[h]), 0.0) - kept
        ).astype(BF16)

    @pl.when(gives & (place > 0))
    def _():
        for g in range(groups):
            gift(1, g).start()

    for h in heads:
        seen = dot_pairs(
            split(attends[h]), split(jnp.concatenate([updates[h], weighted[h]], axis=1))
        )
        local[h] = seen[:, :size]
        asking[h] = (
            jnp.exp(cums[h]) * queries[h].astype(F32) - seen[:, size:]
        ).astype(BF16)

    for i in (5, 7, 6, 8, 9, 10):
        load(i).wait()

    def of_head_col(ref, h):
        block = ref[:, 0, :, h * size : (h + 1) * size]
        return block.reshape(total_rows * width, size)

    def column_gates(ref):
        return jnp.concatenate([ref[t, 0] for t in range(total_rows)], axis=1)

    def column_terms():
        col_solved, col_attends, _, _, _, col_betas, _, _ = prepare(
            [of_head_col(query_col, h) for h in heads],
            [of_head_col(key_col, h) for h in heads],
            column_gates(decay_col),
            column_gates(beta_col),
            width,
            False,
        )
        for h in heads:
            mixer[0, h], mixer[1, h] = split(
                dot_pairs(split(col_attends[h]), split(col_solved[h] * col_betas[h]))
            )

    pl.when(place >= 2)(column_terms)

    @pl.when(place == 0)
    def _():
        state[...] = jnp.zeros_like(state)

    @pl.when(odd == 1)
    def _():
        for g in range(groups):
            gift(0, g).wait_recv()

            @pl.when(place == 1)
            def _():
                state[g] = gift_in[0, g]

            @pl.when(place > 1)
            def _():
                gift(1, g).wait_recv()
                chain(g, 1).wait_recv()
                for j in range(group_heads):
                    state[g, j] = (
                        dot(gift_in[1, g, j], chain_in[g, j]) + gift_in[0, g, j].astype(F32)
                    ).astype(BF16)

            @pl.when(place < scans - 1)
            def _():
                for j in range(group_heads):
                    chain_out[g, j] = (
                        dot(gift_out[1, g, j], state[g, j]) + offset[g * group_heads + j]
                    ).astype(BF16)
                chain(g, 1).start()
                pl.when(place < scans - 2)(lambda: chain(g, 2).start())

    @pl.when((odd == 0) & (place > 0))
    def _():
        for g in range(groups):
            chain(g, 1).wait_recv()
            state[g] = chain_in[g]

    def swap(source, target, send, recv, g, i):
        peer = lax.rem(me + 1 + i, lines)
        return pltpu.make_async_remote_copy(
            src_ref=source.at[g, peer],
            dst_ref=target.at[g, me],
            send_sem=send.at[g, i],
            recv_sem=recv.at[g, me],
            device_id={"line": peer},
            device_id_type=mesh_id,
        )

    def receive(source, target, send, recv, g, i):
        peer = lax.rem(me + 1 + i, lines)
        pltpu.make_async_remote_copy(
            src_ref=source.at[g, peer],
            dst_ref=target.at[g, peer],
            send_sem=send.at[g, i],
            recv_sem=recv.at[g, peer],
            device_id={"line": peer},
            device_id_type=mesh_id,
        ).wait_recv()

    there = (outgoing, incoming, there_send, there_recv)
    back = (returning, returned, back_send, back_recv)

    for g in range(groups):
        for j in range(group_heads):
            h = g * group_heads + j
            row_out = local[h] + dot(asking[h], state[g, j])
            values = normed(row_out, gain_row[...]).astype(BF16)
            outgoing[g, :, j] = values.reshape(lines, tokens // lines, size)
        each(lines - 1, lambda i: swap(*there, g, i).start())
        incoming[g, me] = outgoing[g, me]

    pl.when(place < 2)(column_terms)

    for g in range(groups):
        each(lines - 1, lambda i: receive(*there, g, i))
        for j in range(group_heads):
            h = g * group_heads + j
            values = incoming[g, :, j].reshape(total_rows * width, size)
            mixed = normed(
                dot(mixer[0, h], values) + dot(mixer[1, h], values), gain_col[...]
            ).astype(BF16)
            returning[g, :, j] = mixed.reshape(total_rows, width, size)
        each(lines - 1, lambda i: swap(*back, g, i).start())
        returned[g, me] = returning[g, me]

    for g in range(groups):
        each(lines - 1, lambda i: receive(*back, g, i))
        for j in range(group_heads):
            h = g * group_heads + j
            out[0, :, h * size : (h + 1) * size] = returned[g, :, j].reshape(tokens, size)

    for g in range(groups):
        each(lines - 1, lambda i: swap(*there, g, i).wait_send())
        each(lines - 1, lambda i: swap(*back, g, i).wait_send())

    @pl.when(gives)
    def _():
        for g in range(groups):
            gift(0, g).wait_send()
            pl.when(place > 0)(lambda: gift(1, g).wait_send())

    @pl.when((odd == 1) & (place < scans - 1))
    def _():
        for g in range(groups):
            chain(g, 1).wait_send()
            pl.when(place < scans - 2)(lambda: chain(g, 2).wait_send())


def shards(*arrays):
    query_row, gain_row = arrays[0], arrays[5]
    lines, scans = lax.axis_size("line"), lax.axis_size("scan")
    tokens, features = query_row.shape[1:]
    size = gain_row.shape[0]
    heads = features // size
    groups = 2 if heads % 2 == 0 else 1
    arrays = list(arrays)
    arrays[5] = arrays[5].reshape(1, size)
    arrays[10] = arrays[10].reshape(1, size)
    for i in (3, 4):
        arrays[i] = arrays[i].transpose(0, 2, 1)
    for i in (8, 9):
        arrays[i] = arrays[i].transpose(0, 1, 3, 2)
    grouped = (groups, heads // groups, size, size)
    swapped = (groups, lines, heads // groups, tokens // lines, size)
    dma = pltpu.SemaphoreType.DMA
    return pl.pallas_call(
        functools.partial(kernel, lines, scans),
        out_shape=jax.ShapeDtypeStruct(query_row.shape, BF16),
        in_specs=[pl.BlockSpec(memory_space=pltpu.HBM)] * len(arrays),
        out_specs=pl.BlockSpec(memory_space=pltpu.VMEM),
        scratch_shapes=[pltpu.VMEM(a.shape, a.dtype) for a in arrays]
        + [
            pltpu.VMEM(grouped, BF16),
            pltpu.VMEM((2,) + grouped, BF16),
            pltpu.VMEM((2,) + grouped, BF16),
            pltpu.VMEM(grouped, BF16),
            pltpu.VMEM(grouped, BF16),
            pltpu.VMEM((heads, size, size), F32),
            pltpu.VMEM((heads, tokens, size), F32),
            pltpu.VMEM((heads, tokens, size), BF16),
            pltpu.VMEM((2, heads, tokens, tokens), BF16),
            pltpu.VMEM(swapped, BF16),
            pltpu.VMEM(swapped, BF16),
            pltpu.VMEM(swapped, BF16),
            pltpu.VMEM(swapped, BF16),
            dma((len(arrays),)),
            dma((2, groups)),
            dma((2, groups)),
            dma((2, groups)),
            dma((groups,)),
            dma((groups, lines)),
            dma((groups, lines)),
            dma((groups, lines)),
            dma((groups, lines)),
        ],
        compiler_params=pltpu.CompilerParams(
            collective_id=0, has_side_effects=True, vmem_limit_bytes=60 * 1024 * 1024
        ),
    )(*arrays)


def solution(mesh):
    placed = (
        P("line", "scan", None),
        P("line", "scan", None),
        P("line", "scan", None),
        P("line", "scan", None),
        P("line", "scan", None),
        P(),
        P(None, "scan", "line", None),
        P(None, "scan", "line", None),
        P(None, "scan", "line", None),
        P(None, "scan", "line", None),
        P(),
    )
    return jax.shard_map(
        shards, mesh=mesh, in_specs=placed, out_specs=P("line", "scan", None), check_vma=False
    )
```

time: 29.6 us -> 25.8 us (0.87)
  local copies, waits for them, and re-layouts: 5.22 us -> 1.57 us
    unnamed x13 -> x1, local copies, waits for them, and re-layouts: 5.22 us -> 1.57 us
where the time goes in v3:
time: 25.8 us; the launch traced here: 25.6 us
  Pallas kernels  24.1 us (93%)
  local copies, waits for them, and re-layouts  1.57 us (6%)
    pallas_call x1, Pallas kernels, shards(): pl.pallas_call(functools.partial(kernel, lines, scans), out_shape=jax.Sha...  24.1 us
    unnamed x1, local copies, waits for them, and re-layouts  1.57 us

profile of v3, /device:TPU:5, one launch (start us, length us, event | category | flops | bytes accessed | tf_op | source)
XLA Modules:
  0.0 25.6 jit_solution(9023065562365122629)
XLA Ops:
  0.0 24.1 %shard_map.109 = bf16[1,128,512]{2,1,0:T(8,128)(2,1)} custom-call(bf16[1,128,512]{2,1,0:T(8,128)(2,1)} %refs_0_.1, bf16[1,128,512]{2,1,0:T(8,128)(2,1)} %refs_1_.1, bf16[1,128,512]{2,1,0:T(8,128)(2,1)} %refs_2_.1, f32[1,4,128]{2,1,0:T(4,128)} %bitcast.8, f32[1,4,128]{2,1,0:T(4,128)} %bitcast.9, f32[1,128]{1,0:T(1,128)} %bitcast.10, ...), custom_call_target="tpu_custom_call" | custom-call | tf_op jit(solution)/shard_map/pallas_call | solution.py:435
  24.1 1.6 %copy.13 = bf16[1,128,512]{2,1,0:T(8,128)(2,1)} copy(bf16[1,128,512]{2,1,0:T(8,128)(2,1)} %shard_map.109) | data formatting | bytes 262144

commit v4 on v3

--- a/solution.py
+++ b/solution.py
@@ -311,9 +311,9 @@
     def _():
         state[...] = jnp.zeros_like(state)
 
-    @pl.when(odd == 1)
-    def _():
-        for g in range(groups):
+    def receive_state(g):
+        @pl.when(odd == 1)
+        def _():
             gift(0, g).wait_recv()
 
             @pl.when(place == 1)
@@ -338,9 +338,8 @@
                 chain(g, 1).start()
                 pl.when(place < scans - 2)(lambda: chain(g, 2).start())
 
-    @pl.when((odd == 0) & (place > 0))
-    def _():
-        for g in range(groups):
+        @pl.when((odd == 0) & (place > 0))
+        def _():
             chain(g, 1).wait_recv()
             state[g] = chain_in[g]
 
@@ -370,6 +369,7 @@
     back = (returning, returned, back_send, back_recv)
 
     for g in range(groups):
+        receive_state(g)
         for j in range(group_heads):
             h = g * group_heads + j
             row_out = local[h] + dot(asking[h], state[g, j])
@@ -421,7 +421,7 @@
     tokens, features = query_row.shape[1:]
     size = gain_row.shape[0]
     heads = features // size
-    groups = 2 if heads % 2 == 0 else 1
+    groups = heads
     arrays = list(arrays)
     arrays[5] = arrays[5].reshape(1, size)
     arrays[10] = arrays[10].reshape(1, size)
@@ -434,7 +434,7 @@
     dma = pltpu.SemaphoreType.DMA
     return pl.pallas_call(
         functools.partial(kernel, lines, scans),
-        out_shape=jax.ShapeDtypeStruct(query_row.shape, BF16),
+        out_shape=pltpu.VMEM(query_row.shape, BF16),
         in_specs=[pl.BlockSpec(memory_space=pltpu.HBM)] * len(arrays),
         out_specs=pl.BlockSpec(memory_space=pltpu.VMEM),
         scratch_shapes=[pltpu.VMEM(a.shape, a.dtype) for a in arrays]

time: 25.8 us -> 23.2 us (0.90)
  Pallas kernels: 24.1 us -> 22.4 us
  local copies, waits for them, and re-layouts: 1.57 us -> 0.66 us
    pallas_call x1, Pallas kernels: 24.1 us -> 22.4 us  [shards(): pl.pallas_call(functools.partial(kernel, lines, scans), out_shape=pltpu.V...]
    unnamed x1, local copies, waits for them, and re-layouts: 1.57 us -> 0.66 us
where the time goes in v4:
time: 23.2 us; the launch traced here: 23.1 us
  Pallas kernels  22.4 us (97%)
  local copies, waits for them, and re-layouts  0.66 us (3%)
    pallas_call x1, Pallas kernels, shards(): pl.pallas_call(functools.partial(kernel, lines, scans), out_shape=pltpu.V...  22.4 us
    unnamed x1, local copies, waits for them, and re-layouts  0.66 us

profile of v4, /device:TPU:5, one launch (start us, length us, event | category | flops | bytes accessed | tf_op | source)
XLA Modules:
  0.0 23.1 jit_solution(16970007719844355130)
XLA Ops:
  0.0 22.4 %shard_map.109 = bf16[1,128,512]{2,1,0:T(8,128)(2,1)S(1)} custom-call(bf16[1,128,512]{2,1,0:T(8,128)(2,1)} %refs_0_.1, bf16[1,128,512]{2,1,0:T(8,128)(2,1)} %refs_1_.1, bf16[1,128,512]{2,1,0:T(8,128)(2,1)} %refs_2_.1, f32[1,4,128]{2,1,0:T(4,128)} %bitcast.8, f32[1,4,128]{2,1,0:T(4,128)} %bitcast.9, f32[1,128]{1,0:T(1,128)} %bitcast.10, ...), custom_call_target="tpu_custom_call" | custom-call | tf_op jit(solution)/shard_map/pallas_call | solution.py:435
  22.4 0.7 %copy.13 = bf16[1,128,512]{2,1,0:T(8,128)(2,1)} copy(bf16[1,128,512]{2,1,0:T(8,128)(2,1)S(1)} %shard_map.109) | data formatting | bytes 262144

commit v5 on v4

--- a/solution.py
+++ b/solution.py
@@ -250,14 +250,21 @@
     lasts = [c[tokens - 1 : tokens, :] for c in cums]
     tails = [jnp.exp(lasts[h] - cums[h]) * units[h] for h in heads]
     keys_t = [k.astype(F32).T.astype(BF16) for k in keys]
-    updates, weighted = {}, {}
-    for g in range(groups):
-        for j in range(group_heads):
-            h = g * group_heads + j
-            updates[h] = dot_left(solved[h] * beta_rows[h], of_head(value_row, h))
-            offset[h] = dot(keys_t[h], (tails[h] * updates[h]).astype(BF16))
-            gift_out[0, g, j] = offset[h].astype(BF16)
-        pl.when(gives)(lambda: gift(0, g).start())
+    updates = [
+        dot_left(solved[h] * beta_rows[h], of_head(value_row, h)) for h in heads
+    ]
+    offsets = [dot(keys_t[h], (tails[h] * updates[h]).astype(BF16)) for h in heads]
+    for h in heads:
+        gift_out[0, h // group_heads, h % group_heads] = offsets[h].astype(BF16)
+
+    @pl.when(gives)
+    def _():
+        for g in range(groups):
+            gift(0, g).start()
+
+    weighted = {}
+    for h in heads:
+        offset[h] = offsets[h]
     for h in heads:
         weighted[h] = dot_left(
             solved[h] * (beta_rows[h] * jnp.exp(cum_rows[h]) * unit_rows[h]), keys[h]

time: 23.2 us -> 23.3 us (level)
  no operation moved by 1% of the time
where the time goes in v5:
time: 23.3 us; the launch traced here: 23.2 us
  Pallas kernels  22.5 us (97%)
  local copies, waits for them, and re-layouts  0.66 us (3%)
    pallas_call x1, Pallas kernels, shards(): pl.pallas_call(functools.partial(kernel, lines, scans), out_shape=pltpu.V...  22.5 us
    unnamed x1, local copies, waits for them, and re-layouts  0.66 us

profile of v5, /device:TPU:5, one launch (start us, length us, event | category | flops | bytes accessed | tf_op | source)
XLA Modules:
  0.0 23.2 jit_solution(14050697853478702950)
XLA Ops:
  0.0 22.5 %shard_map.109 = bf16[1,128,512]{2,1,0:T(8,128)(2,1)S(1)} custom-call(bf16[1,128,512]{2,1,0:T(8,128)(2,1)} %refs_0_.1, bf16[1,128,512]{2,1,0:T(8,128)(2,1)} %refs_1_.1, bf16[1,128,512]{2,1,0:T(8,128)(2,1)} %refs_2_.1, f32[1,4,128]{2,1,0:T(4,128)} %bitcast.8, f32[1,4,128]{2,1,0:T(4,128)} %bitcast.9, f32[1,128]{1,0:T(1,128)} %bitcast.10, ...), custom_call_target="tpu_custom_call" | custom-call | tf_op jit(solution)/shard_map/pallas_call | solution.py:442
  22.5 0.7 %copy.13 = bf16[1,128,512]{2,1,0:T(8,128)(2,1)} copy(bf16[1,128,512]{2,1,0:T(8,128)(2,1)S(1)} %shard_map.109) | data formatting | bytes 262144

commit v6 on v5

--- a/solution.py
+++ b/solution.py
@@ -15,10 +15,6 @@
     return jnp.dot(a, b, preferred_element_type=F32)
 
 
-def dot_t(a, b):
-    return lax.dot_general(a, b, (((1,), (1,)), ((), ())), preferred_element_type=F32)
-
-
 def split(a):
     high = a.astype(BF16)
     return high, (a - high.astype(F32)).astype(BF16)
@@ -53,7 +49,7 @@
     return dot(a.astype(BF16), b.astype(BF16))
 
 
-def inverse(systems, row, col, diagonal, stride, steps, refine):
+def inverse(systems, row, col, diagonal, stride, steps):
     unit = jnp.where(diagonal, 1.0, 0.0)
     base = min(16, steps)
     near = (row // (base * stride)) == (col // (base * stride))
@@ -73,15 +69,10 @@
         inner = [dot16(jnp.where(link, m, 0.0), t) for m, t in zip(systems, total)]
         total = [t - dot16(t, i) for t, i in zip(total, inner)]
         size *= 2
-    if refine:
-        left = [
-            (unit - t) - dot_pairs(split(m), split(t)) for m, t in zip(systems, total)
-        ]
-        total = [t + dot16(t, e) for t, e in zip(total, left)]
     return total
 
 
-def prepare(queries, keys, decay, beta, stride, refine):
+def prepare(keys, keys_t, decay, beta, stride):
     size = keys[0].shape[0]
     steps = size // stride
     count = len(keys)
@@ -98,9 +89,9 @@
     cum_rows = [cumulative[h : h + 1] for h in range(count)]
     beta_rows = [beta[h : h + 1] for h in range(count)]
     cums = [packed[:, h : h + 1] for h in range(count)]
-    systems, attends, units, unit_rows = [], [], [], []
+    systems, ratios, units, unit_rows = [], [], [], []
     for h in range(count):
-        gram = dot_t(keys[h], keys[h])
+        gram = dot(keys[h], keys_t[h])
         squares = jnp.where(diagonal, gram, 0.0)
         unit_col = lax.rsqrt(jnp.sum(squares, axis=1, keepdims=True) + 1e-06)
         unit_row = lax.rsqrt(jnp.sum(squares, axis=0, keepdims=True) + 1e-06)
@@ -108,11 +99,11 @@
         ratio = jnp.where(lower, jnp.exp(jnp.where(lower, spread, 0.0)), 0.0) * unit_row
         beta_col = packed[:, count + h : count + h + 1]
         systems.append(jnp.where(strict, (beta_col * unit_col) * (ratio * gram), 0.0))
-        attends.append(ratio * dot_t(queries[h], keys[h]))
+        ratios.append(ratio)
         units.append(unit_col)
         unit_rows.append(unit_row)
-    solved = inverse(systems, row, col, diagonal, stride, steps, refine)
-    return solved, attends, cums, units, cum_rows, beta_rows, unit_rows, diagonal
+    solved = inverse(systems, row, col, diagonal, stride, steps)
+    return solved, ratios, cums, units, cum_rows, beta_rows, unit_rows, diagonal
 
 
 def normed(block, gain):
@@ -209,12 +200,12 @@
     def of_head(ref, h):
         return ref[0, :, h * size : (h + 1) * size]
 
-    for i in (1, 3, 4, 0):
+    for i in (1, 3, 4):
         load(i).wait()
-    queries = [of_head(query_row, h) for h in heads]
     keys = [of_head(key_row, h) for h in heads]
-    solved, attends, cums, units, cum_rows, beta_rows, unit_rows, diagonal = prepare(
-        queries, keys, decay_row[0], beta_row[0], 1, True
+    keys_t = [k.T for k in keys]
+    solved, ratios, cums, units, cum_rows, beta_rows, unit_rows, diagonal = prepare(
+        keys, keys_t, decay_row[0], beta_row[0], 1
     )
     load(2).wait()
     pl.semaphore_wait(
@@ -249,7 +240,6 @@
     gives = (odd == 0) & (place < scans - 1)
     lasts = [c[tokens - 1 : tokens, :] for c in cums]
     tails = [jnp.exp(lasts[h] - cums[h]) * units[h] for h in heads]
-    keys_t = [k.astype(F32).T.astype(BF16) for k in keys]
     updates = [
         dot_left(solved[h] * beta_rows[h], of_head(value_row, h)) for h in heads
     ]
@@ -279,9 +269,11 @@
         for g in range(groups):
             gift(1, g).start()
 
+    load(0).wait()
+    queries = [of_head(query_row, h) for h in heads]
     for h in heads:
         seen = dot_pairs(
-            split(attends[h]), split(jnp.concatenate([updates[h], weighted[h]], axis=1))
+            split(ratios[h] * dot(queries[h], keys_t[h])), split(jnp.concatenate([updates[h], weighted[h]], axis=1))
         )
         local[h] = seen[:, :size]
         asking[h] = (
@@ -299,17 +291,15 @@
         return jnp.concatenate([ref[t, 0] for t in range(total_rows)], axis=1)
 
     def column_terms():
-        col_solved, col_attends, _, _, _, col_betas, _, _ = prepare(
-            [of_head_col(query_col, h) for h in heads],
-            [of_head_col(key_col, h) for h in heads],
-            column_gates(decay_col),
-            column_gates(beta_col),
-            width,
-            False,
+        col_keys = [of_head_col(key_col, h) for h in heads]
+        col_keys_t = [k.T for k in col_keys]
+        col_solved, col_ratios, _, _, _, col_betas, _, _ = prepare(
+            col_keys, col_keys_t, column_gates(decay_col), column_gates(beta_col), width
         )
         for h in heads:
+            attend = col_ratios[h] * dot(of_head_col(query_col, h), col_keys_t[h])
             mixer[0, h], mixer[1, h] = split(
-                dot_pairs(split(col_attends[h]), split(col_solved[h] * col_betas[h]))
+                dot_pairs(split(attend), split(col_solved[h] * col_betas[h]))
             )
 
     pl.when(place >= 2)(column_terms)

time: 23.3 us -> 22.9 us (0.983)
  Pallas kernels: 22.5 us -> 22.1 us
    pallas_call x1, Pallas kernels: 22.5 us -> 22.1 us  [shards(): pl.pallas_call(functools.partial(kernel, lines, scans), out_shape=pltpu.V...]
where the time goes in v6:
time: 22.9 us; the launch traced here: 22.7 us
  Pallas kernels  22.1 us (97%)
  local copies, waits for them, and re-layouts  0.66 us (3%)
    pallas_call x1, Pallas kernels, shards(): pl.pallas_call(functools.partial(kernel, lines, scans), out_shape=pltpu.V...  22.1 us
    unnamed x1, local copies, waits for them, and re-layouts  0.66 us

profile of v6, /device:TPU:5, one launch (start us, length us, event | category | flops | bytes accessed | tf_op | source)
XLA Modules:
  0.0 22.7 jit_solution(3785667650405442810)
XLA Ops:
  0.0 22.1 %shard_map.109 = bf16[1,128,512]{2,1,0:T(8,128)(2,1)S(1)} custom-call(bf16[1,128,512]{2,1,0:T(8,128)(2,1)} %refs_0_.1, bf16[1,128,512]{2,1,0:T(8,128)(2,1)} %refs_1_.1, bf16[1,128,512]{2,1,0:T(8,128)(2,1)} %refs_2_.1, f32[1,4,128]{2,1,0:T(4,128)} %bitcast.8, f32[1,4,128]{2,1,0:T(4,128)} %bitcast.9, f32[1,128]{1,0:T(1,128)} %bitcast.10, ...), custom_call_target="tpu_custom_call" | custom-call | tf_op jit(solution)/shard_map/pallas_call | solution.py:432
  22.1 0.7 %copy.13 = bf16[1,128,512]{2,1,0:T(8,128)(2,1)} copy(bf16[1,128,512]{2,1,0:T(8,128)(2,1)S(1)} %shard_map.109) | data formatting | bytes 262144

commit v7 on v6

--- a/solution.py
+++ b/solution.py
@@ -365,8 +365,15 @@
     there = (outgoing, incoming, there_send, there_recv)
     back = (returning, returned, back_send, back_recv)
 
+    forwards = (odd == 1) & (place < scans - 1)
+
+    @pl.when(forwards)
+    def _():
+        for g in range(groups):
+            receive_state(g)
+
     for g in range(groups):
-        receive_state(g)
+        pl.when(jnp.logical_not(forwards))(functools.partial(receive_state, g))
         for j in range(group_heads):
             h = g * group_heads + j
             row_out = local[h] + dot(asking[h], state[g, j])

time: 22.9 us -> 22.9 us (level)
  no operation moved by 1% of the time
where the time goes in v7:
time: 22.9 us; the launch traced here: 22.7 us
  Pallas kernels  22.1 us (97%)
  local copies, waits for them, and re-layouts  0.66 us (3%)
    pallas_call x1, Pallas kernels, shards(): pl.pallas_call(functools.partial(kernel, lines, scans), out_shape=pltpu.V...  22.1 us
    unnamed x1, local copies, waits for them, and re-layouts  0.66 us

profile of v7, /device:TPU:5, one launch (start us, length us, event | category | flops | bytes accessed | tf_op | source)
XLA Modules:
  0.0 22.7 jit_solution(3731974973573950063)
XLA Ops:
  0.0 22.1 %shard_map.109 = bf16[1,128,512]{2,1,0:T(8,128)(2,1)S(1)} custom-call(bf16[1,128,512]{2,1,0:T(8,128)(2,1)} %refs_0_.1, bf16[1,128,512]{2,1,0:T(8,128)(2,1)} %refs_1_.1, bf16[1,128,512]{2,1,0:T(8,128)(2,1)} %refs_2_.1, f32[1,4,128]{2,1,0:T(4,128)} %bitcast.8, f32[1,4,128]{2,1,0:T(4,128)} %bitcast.9, f32[1,128]{1,0:T(1,128)} %bitcast.10, ...), custom_call_target="tpu_custom_call" | custom-call | tf_op jit(solution)/shard_map/pallas_call | solution.py:439
  22.1 0.7 %copy.13 = bf16[1,128,512]{2,1,0:T(8,128)(2,1)} copy(bf16[1,128,512]{2,1,0:T(8,128)(2,1)S(1)} %shard_map.109) | data formatting | bytes 262144
